TPU v7x, 128 devices: a whole 4x4x4 slice. The times are simulated.
128 devices in a mesh: blk: 128 (over x, z, y, core).
Axes of the slice: x: 4, y: 4, z: 4, core: 2. Of those that a mesh axis runs over, the one named last changes fastest.
Arguments:
- x_points: bfloat16 [262144, 512], P('blk'), may hold values from -0.375 to 0.375
- y_points: bfloat16 [262144, 512], P('blk'), may hold values from -0.375 to 0.375
- x_start: bfloat16 [262144], P('blk'), may hold values from -1 to 16
- y_start: bfloat16 [262144], P('blk'), may hold values from -1 to 16
- x_order: int32 [262144], P('blk'), may hold values from 0 to 262143, as said below
- y_order: int32 [262144], P('blk'), may hold values from 0 to 262143, as said below
- partners: int32 [256, 6], P('blk'), may hold values from 0 to 255, as said below
- counts: int32 [256], P('blk'), may hold values from 1 to 6, as said below
Outputs:
- f_out: float32 [262144], P('blk')
- g_out: float32 [262144], P('blk')
Inputs may be any that keep to these rules, and one draw needn't show every extreme that they name: x_order is a permutation; every device's points are sent in equal numbers, 2 * 1024 / 128, to the cluster positions of every device. y_order is a permutation; every device's points are sent in equal numbers, 2 * 1024 / 128, to the cluster positions of every device. `partners`: slot 0 of row b is b itself; the first counts[b] slots of row b are distinct blocks held by devices within 3 of the device that holds block b; of the blocks held by any one other device, the rows of all blocks held by one device name at most one; the other slots repeat b. `counts`: 6 is reached in every draw.
All inputs are finite; a program needn't handle non-finite values.
Results may differ from a plain program's by a relative error of at most 0.0003.
Values may be sent and summed in bfloat16 or wider, within the bound.
No kernel may reach another device: no remote copies, remote signals or barrier semaphores. Data moves between devices by JAX's collectives and lax.ppermute only.
A program may use at most 128 MiB of HBM per device.

v0:
```python
import functools
import math

import jax
import jax.numpy as jnp
import numpy as np
from jax import lax
from jax.experimental import pallas as pl
from jax.experimental.pallas import tpu as pltpu
from jax.sharding import PartitionSpec as P

DIM = 512
BS = 1024
BPD = 2
REACH = 3
LOCAL = BPD * BS
EXTRA = 128
WIDE = 2 * DIM + EXTRA
TAIL = 16
ROWS = BS + TAIL
CHUNK = 512
PART = 256
ROUNDS = ((1, 2, -2, 3, -3, -1), (-1, 2, -2, -3, 3, 1), (1, -2, 2, 3, -3, -1), (-1, -2, 2, -3, 3, 1))
FAR = len(ROUNDS[0])
YBLOCKS = BPD + FAR
SLOTS = BPD * YBLOCKS
MOST = 12
GROUP = 8
PEERS = 2 * GROUP
X_LANES = EXTRA // 2

entropy_weight = 0.05
scale = math.log2(math.e) / entropy_weight
log_two = math.log(2.0)
lowest = -1e30
exponent_room = 112.0
mebi = 1024 * 1024

f32 = jnp.float32
bf16 = jnp.bfloat16
i32 = jnp.int32

SMEM = pl.BlockSpec(memory_space=pltpu.SMEM)
ANY = pl.BlockSpec(memory_space=pl.ANY)
VMEM = pl.BlockSpec(memory_space=pltpu.VMEM)
HBM = pl.BlockSpec(memory_space=pltpu.HBM)


def iota(shape, dim):
    return lax.broadcasted_iota(i32, shape, dim)


def dot(a, b):
    return jnp.dot(a, b, preferred_element_type=f32)


def nt_dot(a, b):
    return lax.dot_general(a, b, (((1,), (1,)), ((), ())), preferred_element_type=f32)


def ones_where(mask):
    return jnp.where(mask, 1.0, 0.0).astype(bf16)


def params():
    return pltpu.CompilerParams(vmem_limit_bytes=62 * mebi)


def whole(shape):
    return pl.BlockSpec(shape, lambda *t: (0,) * len(shape))


def laid_out(square):
    return jnp.concatenate([square[n : n + 1, :] for n in range(square.shape[0])], axis=1)


def down(row):
    parts = [jnp.broadcast_to(row[:, c : c + 128], (128, 128)).T for c in range(0, row.shape[1], 128)]
    return jnp.concatenate(parts, axis=0)


def moved(values, place):
    high = iota((16, LOCAL), 0) == lax.shift_right_logical(place, 7)
    low = ones_where(iota((128, LOCAL), 0) == jnp.bitwise_and(place, 127))
    stack = jnp.concatenate([jnp.where(high, v, 0.0) for v in values], axis=0).astype(bf16)
    out = nt_dot(stack, low)
    return [laid_out(out[16 * n : 16 * n + 16, :]) for n in range(len(values))]


def moved_exact(value, place):
    first = value.astype(bf16).astype(f32)
    second = (value - first).astype(bf16).astype(f32)
    parts = moved([first, second, value - first - second], place)
    return parts[0] + parts[1] + parts[2]


def before_matrix():
    return ones_where(iota((128, 128), 0) < iota((128, 128), 1))


def plan(order, start, devices, first_lane):
    share = LOCAL // devices
    target = lax.shift_right_logical(order, 11)
    hit = iota((devices, LOCAL), 0) == target
    hot = ones_where(hit)
    before = before_matrix()
    every = jnp.ones((128, 128), bf16)
    seen = jnp.zeros((devices, 128), f32)
    earlier = []
    for c in range(0, LOCAL, 128):
        piece = hot[:, c : c + 128]
        earlier.append(dot(piece, before) + seen)
        seen = seen + dot(piece, every)
    earlier = jnp.concatenate(earlier, axis=1)
    rank = jnp.sum(jnp.where(hit, earlier, 0.0), axis=0, keepdims=True).astype(i32)
    within = jnp.bitwise_and(order, LOCAL - 1)
    high = lax.shift_right_logical(within, 6).astype(f32)
    low = jnp.bitwise_and(within, 63).astype(f32)
    row = iota((EXTRA, LOCAL), 0) - first_lane
    field = row // share
    value = jnp.where(field == 0, high, jnp.where(field == 1, low, start))
    mine = (row >= 0) & (row < 3 * share) & (row % share == rank)
    return target * share + rank, nt_dot(hot, jnp.where(mine, value, 0.0).astype(bf16))


def partner_offsets(me):
    kind = jnp.bitwise_and(me, 3)
    out = []
    for k in range(FAR):
        value = jnp.int32(ROUNDS[0][k])
        for n in range(1, 4):
            value = jnp.where(kind == n, jnp.int32(ROUNDS[n][k]), value)
        out.append(value)
    return out


def pack_kernel(
    me_ref, partners_ref, counts_ref, y_order, x_order, y_start, x_start, y_points, x_points, out_ref, pos_ref, table_ref,
    *, devices
):
    step = pl.program_id(0)
    share = LOCAL // devices

    @pl.when(step == 0)
    def _():
        y_pos, y_table = plan(y_order[...], y_start[...].astype(f32).reshape(1, LOCAL), devices, 0)
        x_pos, x_table = plan(x_order[...], x_start[...].astype(f32).reshape(1, LOCAL), devices, X_LANES)
        pos_ref[0:1, :] = y_pos
        pos_ref[1:2, :] = x_pos
        me = me_ref[0]
        offsets = partner_offsets(me)
        need = [jnp.int32(0)] * FAR
        for b in range(BPD):
            for s in range(partners_ref.shape[1]):
                block = partners_ref[b, s]
                away = lax.shift_right_logical(block, 1) - me
                for k in range(FAR):
                    listed = (s < counts_ref[b]) & (away == offsets[k])
                    need[k] = jnp.where(listed, jnp.bitwise_and(block, 1), need[k])
        table = y_table + x_table
        row, lane = iota(table.shape, 0), iota(table.shape, 1)
        for k in range(FAR):
            table = jnp.where((row == me + offsets[k]) & (lane == 3 * share), need[k].astype(f32), table)
        table_ref[...] = table

    base = step * CHUNK
    for n, points in enumerate((y_points, x_points)):
        hot = ones_where(iota((CHUNK, LOCAL), 0) + base == pos_ref[n : n + 1, :])
        out_ref[:, n * DIM : (n + 1) * DIM] = dot(hot, points[...]).astype(bf16)
    some = CHUNK // share
    table = table_ref[pl.ds(pl.multiple_of(step * some, some), some), :]
    out_ref[:, 2 * DIM :] = jnp.broadcast_to(table[:, None, :], (some, share, EXTRA)).reshape(CHUNK, EXTRA).astype(bf16)


def pack(me, partners, counts, y_order, x_order, y_start, x_start, y_points, x_points, devices):
    row = whole((1, LOCAL))
    return pl.pallas_call(
        functools.partial(pack_kernel, devices=devices),
        grid=(LOCAL // CHUNK,),
        in_specs=[SMEM, SMEM, SMEM, row, row, whole((LOCAL,)), whole((LOCAL,)), whole((LOCAL, DIM)), whole((LOCAL, DIM))],
        out_specs=pl.BlockSpec((CHUNK, WIDE), lambda t: (t, 0)),
        out_shape=pltpu.HBM((LOCAL, WIDE), bf16),
        scratch_shapes=[pltpu.VMEM((8, LOCAL), i32), pltpu.VMEM((devices, EXTRA), f32)],
        compiler_params=params(),
        name="pack",
    )(me, partners, counts, y_order, x_order, y_start, x_start, y_points, x_points)


WINDOW = PART + 16
HELD = BS + WINDOW + 16


def arrived(table, base, with_low):
    share = 16
    row, lane = iota((EXTRA, EXTRA), 0), iota((EXTRA, EXTRA), 1)
    pick = jnp.where(row == base + lane % share, 64.0 if with_low else 1.0, 0.0)
    if with_low:
        pick = jnp.where(row == base + share + lane % share, 1.0, pick)
    values = dot(table, pick.astype(bf16))
    values = jnp.where(row % (EXTRA // share) == lane // share, values, 0.0)
    return jnp.sum(values.reshape(LOCAL // 128, EXTRA // share, 128), axis=1)


def unpack_y_kernel(me_ref, came_ref, rows_ref, table_ref, own_ref, *rest, devices):
    sends = rest[:FAR]
    held, sems, own_sem, points_buf, extra_buf, in_sems = rest[FAR:]
    share = LOCAL // devices
    me = me_ref[0]
    extra_in = pltpu.make_async_copy(came_ref.at[:, pl.ds(2 * DIM, EXTRA)], extra_buf, in_sems.at[0])
    points_in = pltpu.make_async_copy(came_ref.at[:, pl.ds(0, DIM)], points_buf, in_sems.at[1])
    extra_in.start()
    points_in.start()
    held[...] = jnp.zeros(held.shape, bf16)
    extra_in.wait()
    table = dot(ones_where(iota((devices, LOCAL), 1) == iota((devices, LOCAL), 0) * share), extra_buf[...])
    table_ref[...] = table
    place_square = arrived(table.astype(bf16), 0, True)
    place = laid_out(place_square)
    start = laid_out(arrived(table.astype(bf16), 2 * share, False))

    picks = []
    offsets = partner_offsets(me)
    small_row, small_lane = iota((devices, EXTRA), 0), iota((devices, EXTRA), 1)
    for k in range(FAR):
        here = (small_row == me + offsets[k]) & (small_lane == 3 * share)
        picks.append(jnp.sum(jnp.where(here, table, 0.0)) > 0.5)

    second = place >= float(BS)
    square = ones_where(place_square >= float(BS))
    totals = dot(square, jnp.ones((128, 128), bf16)).astype(bf16)
    earlier = dot(square, before_matrix()) + dot(ones_where(iota((16, 16), 1) < iota((16, 16), 0)), totals)
    ones_before = laid_out(earlier)
    dest = jnp.where(second, ones_before, iota((1, LOCAL), 1).astype(f32) - ones_before).astype(i32)
    seat = jnp.where(second, dest + BS, dest)
    position = place.astype(i32)
    start_row, high_row, low_row = moved(
        [start, lax.shift_right_logical(position, 6).astype(f32), jnp.bitwise_and(position, 63).astype(f32)], seat
    )
    rows_ref[0:1, :] = start_row
    rows_ref[2:3, :] = high_row * 64.0 + low_row
    rows_ref[3:8, :] = jnp.zeros((5, LOCAL), f32)
    sixteen, lane16 = iota((16, 128), 0), iota((16, 128), 1)
    points_in.wait()

    for j in range(BPD):
        here = jnp.where(second if j else jnp.logical_not(second), dest, -1)
        for c in range(LOCAL // PART):
            span = slice(c * PART, (c + 1) * PART)
            begin = jnp.sum(jnp.where((sixteen == c * PART // 128) & (lane16 == 0), earlier, 0.0)).astype(i32)
            if j == 0:
                begin = c * PART - begin
            begin = pl.multiple_of(lax.shift_left(lax.shift_right_logical(begin, 4), 4), 16)
            hot = ones_where(iota((WINDOW, PART), 0) + begin == here[:, span])
            part = dot(hot, points_buf[span, :]).astype(bf16)
            held[j, pl.ds(begin, WINDOW), :] = held[j, pl.ds(begin, WINDOW), :] + part
        half = []
        for c in range(0, BS, PART):
            points = held[j, c : c + PART, :].astype(f32)
            total = 0.5 * jnp.sum(points * points, axis=1, keepdims=True)
            half.append(jnp.broadcast_to(total, (PART, 128)).T[0:1, :])
        half = jnp.concatenate(half, axis=1)
        block = slice(j * BS, (j + 1) * BS)
        rows_ref[1:2, block] = half
        beta = start_row[:, block] - half
        first = beta.astype(bf16).astype(f32)
        next_part = (beta - first).astype(bf16).astype(f32)
        most = jnp.max(half, axis=1, keepdims=True) * 1.01
        sub = iota((TAIL, DIM), 0)
        tail = jnp.zeros((TAIL, DIM), f32) + most
        for n, piece in enumerate((first, next_part, beta - first - next_part)):
            tail = jnp.where(sub == 2 * n, piece[:, :DIM], tail)
            tail = jnp.where(sub == 2 * n + 1, piece[:, DIM:], tail)
        held[j, BS:ROWS, :] = tail.astype(bf16)
        done = held.at[j, pl.ds(0, ROWS), :]
        for k in range(FAR):
            wanted = picks[k] if j == 1 else jnp.logical_not(picks[k])

            @pl.when(wanted)
            def _():
                pltpu.make_async_copy(done, sends[k], sems.at[k]).start()

        pltpu.make_async_copy(done, own_ref.at[j], own_sem.at[j]).start()

    done = held.at[0, pl.ds(0, ROWS), :]
    for k in range(FAR):
        pltpu.make_async_copy(done, sends[k], sems.at[k]).wait()
    for j in range(BPD):
        pltpu.make_async_copy(done, own_ref.at[j], own_sem.at[j]).wait()


def unpack_y(me, came, devices):
    return pl.pallas_call(
        functools.partial(unpack_y_kernel, devices=devices),
        in_specs=[SMEM, ANY],
        out_specs=[VMEM, VMEM] + [HBM] * (1 + FAR),
        out_shape=[
            jax.ShapeDtypeStruct((8, LOCAL), f32),
            jax.ShapeDtypeStruct((devices, EXTRA), f32),
            pltpu.HBM((BPD, ROWS, DIM), bf16),
        ]
        + [pltpu.HBM((ROWS, DIM), bf16)] * FAR,
        scratch_shapes=[
            pltpu.VMEM((BPD, HELD, DIM), bf16),
            pltpu.SemaphoreType.DMA((FAR,)),
            pltpu.SemaphoreType.DMA((BPD,)),
            pltpu.VMEM((LOCAL, DIM), bf16),
            pltpu.VMEM((LOCAL, EXTRA), bf16),
            pltpu.SemaphoreType.DMA((2,)),
        ],
        compiler_params=params(),
        name="unpack_y",
    )(me, came)


def unpack_x_kernel(came_ref, table_ref, points_ref, alpha_ref, rows_ref, place_ref, start_ref):
    step = pl.program_id(0)

    @pl.when(step == 0)
    def _():
        table = table_ref[...].astype(bf16)
        place = laid_out(arrived(table, X_LANES, True)).astype(i32)
        place_ref[...] = place
        start_ref[...] = moved([laid_out(arrived(table, X_LANES + 32, False))], place)[0]

    base = step * CHUNK
    hot = ones_where(iota((CHUNK, LOCAL), 0) + base == place_ref[...])
    points = dot(hot, came_ref[...])
    points_ref[...] = points.astype(bf16)
    half = jnp.broadcast_to(0.5 * jnp.sum(points * points, axis=1, keepdims=True), (CHUNK, 128))
    start = start_ref[:, pl.ds(pl.multiple_of(base, CHUNK), CHUNK)]
    alpha_ref[...] = (down(start) - half) * scale
    rows_ref[0:1, :] = start
    rows_ref[1:8, :] = jnp.concatenate([half[c : c + 128, :].T[0:7, :] for c in range(0, CHUNK, 128)], axis=1)


def unpack_x(came, table):
    return pl.pallas_call(
        unpack_x_kernel,
        grid=(LOCAL // CHUNK,),
        in_specs=[pl.BlockSpec((LOCAL, DIM), lambda t: (0, 1)), whole((EXTRA, EXTRA))],
        out_specs=[
            pl.BlockSpec((CHUNK, DIM), lambda t: (t, 0)),
            pl.BlockSpec((CHUNK, 128), lambda t: (t, 0)),
            pl.BlockSpec((8, CHUNK), lambda t: (0, t)),
        ],
        out_shape=[
            pltpu.HBM((LOCAL, DIM), bf16),
            pltpu.HBM((LOCAL, 128), f32),
            jax.ShapeDtypeStruct((8, LOCAL), f32),
        ],
        scratch_shapes=[pltpu.VMEM((1, LOCAL), i32), pltpu.VMEM((1, LOCAL), f32)],
        compiler_params=params(),
        name="unpack_x",
    )(came, table)


def merge(top, total, other_top, other_total):
    new = jnp.maximum(top, other_top)
    return new, total * jnp.exp2(top - new) + other_total * jnp.exp2(other_top - new)


def logs(top, total):
    return jnp.where(total > 0.0, top + jnp.log2(total), lowest)


def high_of(row):
    return jnp.max(row, axis=1, keepdims=True)


def low_of(row):
    return jnp.min(row, axis=1, keepdims=True)


def put_cols(col_ref, y, part_top, part_total):
    top, total = merge(col_ref[y, 0:1, :], col_ref[y, 1:2, :], part_top, part_total)
    col_ref[y, 0:1, :] = top
    col_ref[y, 1:2, :] = total


def clear_cols(col_ref):
    col_ref[:, 0:1, :] = jnp.full((col_ref.shape[0], 1, BS), lowest, f32)
    col_ref[:, 1:2, :] = jnp.zeros((col_ref.shape[0], 1, BS), f32)


def shifted_rows(x_ref, y_ref, beta, part_ref):
    def body(c, carry):
        span = pl.ds(pl.multiple_of(c * PART, PART), PART)
        terms = nt_dot(x_ref[span, :], y_ref[0:BS, :]) * scale + beta
        top = jnp.max(terms, axis=1, keepdims=True)
        total = jnp.sum(jnp.exp2(terms - top), axis=1, keepdims=True)
        part_ref[span, :] = jnp.where(iota((PART, 128), 1) == 0, top, total)
        return carry

    lax.fori_loop(0, BS // PART, body, 0)


def shifted_cols(x_ref, y_ref, alpha_ref, col_ref, y):
    def body(c, carry):
        span = pl.ds(pl.multiple_of(c * PART, PART), PART)
        terms = nt_dot(x_ref[span, :], y_ref[0:BS, :]) * scale + alpha_ref[span, 0:1]
        top = jnp.max(terms, axis=0, keepdims=True)
        put_cols(col_ref, y, top, jnp.sum(jnp.exp2(terms - top), axis=0, keepdims=True))
        return carry

    lax.fori_loop(0, BS // PART, body, 0)


def add_part(part_ref, state_ref, b):
    for c in range(0, BS, 128):
        part = part_ref[c : c + 128, :].T
        span = pl.ds(pl.multiple_of(b * BS + c, 128), 128)
        top, total = merge(state_ref[0:1, span], state_ref[1:2, span], part[0:1, :], part[1:2, :])
        state_ref[0:1, span] = top
        state_ref[1:2, span] = total


def lane_sums(refs):
    out = []
    for c in range(0, LOCAL, 128):
        part = refs[0][c : c + 128, :]
        for ref in refs[1:]:
            part = part + ref[c : c + 128, :]
        out.append(jnp.sum(part.T, axis=0, keepdims=True))
    return jnp.concatenate(out, axis=1)


def fold(values):
    return jnp.sum(values.reshape(values.shape[0] // 8, 8, 128), axis=0)


def own_beta(y_rows_ref):
    return (y_rows_ref[0:1, :] - y_rows_ref[1:2, :]) * scale


def sweep_kernel(*refs, base, count, first, last):
    use_ref, seat_of_ref, x_ref, alpha_ref, x_rows_ref, y_rows_ref = refs[:6]
    refs = refs[6:]
    if not first:
        cols_in, left_in = refs[:2]
        refs = refs[4:]
    if last:
        peers_ref = refs[0]
        refs = refs[1:]
    y_refs = refs[:1] if first else refs[:count]
    refs = refs[len(y_refs) :]
    acc_ref, cols_ref, left_ref, kept_ref, slow_ref = refs[:5]
    refs = refs[5:]
    if last:
        group_outs = refs[:2]
        refs = refs[2:]
    y_buf, sems, col_ref, weight_ref, part_ref, stat_ref, tiles, tile_sems, tile_count = refs

    def copy(n):
        source = y_refs[0].at[n] if first else y_refs[n]
        return pltpu.make_async_copy(source, y_buf.at[n % 2], sems.at[n % 2])

    copy(0).start()
    tile_count[0] = 0
    acc_ref[...] = jnp.zeros((LOCAL, 128), f32)

    def tile_copy(at, seat):
        return pltpu.make_async_copy(tiles.at[at], kept_ref.at[seat], tile_sems.at[at])

    if first:
        for n in range(SLOTS):
            left_ref[n] = -1.0
    else:
        for n in range(SLOTS):
            left_ref[n] = left_in[n]
        cols_ref[...] = cols_in[...]
    alpha = (x_rows_ref[0:1, :] - x_rows_ref[1:2, :]) * scale
    alpha_top = high_of(alpha)
    weight_ref[...] = jnp.exp2(alpha_ref[...] - alpha_top)
    lane = iota((8, 128), 1)
    beta_top = high_of(own_beta(y_rows_ref))
    most = high_of(x_rows_ref[1:2, :]) * 1.01
    spread = alpha_top - low_of(alpha)
    stat_ref[...] = jnp.where(lane == 0, alpha_top, jnp.where(lane == 1, spread, jnp.where(lane == 2, most, beta_top)))

    def body(step, carry):
        y, b = step // BPD, step % BPD
        slot = base * BPD + step
        for n in range(count):

            @pl.when(step == BPD * n)
            def _():
                copy(n).wait()
                if n + 1 < count:
                    copy(n + 1).start()

        @pl.when(b == 0)
        def _():
            clear_cols(col_ref)

        now = y_buf.at[y % 2]
        rows_from = b * BS

        @pl.when(use_ref[slot] > 0)
        def _():
            tail = now[BS:ROWS, :].astype(f32)
            halves = [tail[n : n + 1, :] + tail[n + 2 : n + 3, :] + tail[n + 4 : n + 5, :] for n in range(2)]
            beta = jnp.concatenate(halves, axis=1) * scale
            shift = stat_ref[0:1, 3:4]
            left = exponent_room - 2.0 * scale * jnp.sqrt(tail[6:7, 0:1] * stat_ref[0:1, 2:3])
            reach = jnp.maximum(stat_ref[0:1, 1:2], jnp.maximum(high_of(beta) - shift, shift - low_of(beta)))
            fits = (left - reach)[0, 0] >= 0.0

            @pl.when(fits)
            def _():
                left_ref[slot] = left[0, 0]
                done = tile_count[0]
                tile_count[0] = done + 1
                at = done % 2

                @pl.when(done > 1)
                def _():
                    tile_copy(at, 0).wait()

                weight = jnp.exp2(beta - shift)
                sums = jnp.zeros((8, BS), f32)
                for c in range(0, BS, PART):
                    span = pl.ds(pl.multiple_of(rows_from + c, PART), PART)
                    terms = jnp.exp2(nt_dot(x_ref[span, :], now[0:BS, :]) * scale)
                    tiles[at, c : c + PART, :] = terms.astype(bf16)
                    row_part = acc_ref[span, :]
                    col_parts = []
                    for n in range(0, BS, 128):
                        piece = terms[:, n : n + 128]
                        row_part = row_part + piece * weight[:, n : n + 128]
                        col_parts.append(fold(piece * weight_ref[span, :]))
                    acc_ref[span, :] = row_part
                    sums = sums + jnp.concatenate(col_parts, axis=1)
                tile_copy(at, seat_of_ref[slot]).start()
                put_cols(col_ref, 0, stat_ref[0:1, 0:1], jnp.sum(sums, axis=0, keepdims=True))

            @pl.when(jnp.logical_not(fits))
            def _():
                block = pl.ds(pl.multiple_of(rows_from, BS), BS)
                shifted_rows(x_ref.at[block, :], now, beta, part_ref)
                out = pltpu.make_async_copy(part_ref, slow_ref.at[slot], sems.at[2])
                out.start()
                shifted_cols(x_ref.at[block, :], now, alpha_ref.at[block, :], col_ref, 0)
                out.wait()

        @pl.when(b == BPD - 1)
        def _():
            cols_ref[base + y] = logs(col_ref[0, 0:1, :], col_ref[0, 1:2, :])

        return carry

    lax.fori_loop(0, BPD * count, body, 0)
    for n in range(2):

        @pl.when(tile_count[0] > n)
        def _():
            tile_copy(n, 0).wait()

    if last:
        for n in range(PEERS):
            group_outs[n // GROUP][n % GROUP] = outgoing(cols_ref, peers_ref[n])


def outgoing(cols_ref, index):
    return jnp.where(index < 0, lowest, cols_ref[jnp.maximum(index, 0)])


def sweep(common, y_list, base, carried, peers):
    first, last = carried is None, peers is not None
    count = BPD if first else len(y_list)
    in_specs = [SMEM, SMEM] + [VMEM] * 4
    operands = list(common)
    aliases = {}
    if not first:
        in_specs += [VMEM, SMEM, HBM, HBM]
        operands += list(carried)
        aliases = {8: 3, 9: 4}
    if last:
        in_specs.append(SMEM)
        operands.append(peers)
    in_specs += [ANY] * len(y_list)
    operands += y_list
    out_specs = [VMEM, VMEM, SMEM, HBM, HBM]
    out_shape = [
        jax.ShapeDtypeStruct((LOCAL, 128), f32),
        jax.ShapeDtypeStruct((YBLOCKS, 1, BS), f32),
        jax.ShapeDtypeStruct((SLOTS,), f32),
        pltpu.HBM((MOST, BS, BS), bf16),
        pltpu.HBM((SLOTS, BS, 128), f32),
    ]
    if last:
        out_specs += [VMEM] * 2
        out_shape += [jax.ShapeDtypeStruct((GROUP, 1, BS), f32)] * 2
    return pl.pallas_call(
        functools.partial(sweep_kernel, base=base, count=count, first=first, last=last),
        in_specs=in_specs,
        out_specs=out_specs,
        out_shape=out_shape,
        scratch_shapes=[
            pltpu.VMEM((2, ROWS, DIM), bf16),
            pltpu.SemaphoreType.DMA((3,)),
            pltpu.VMEM((1, 8, BS), f32),
            pltpu.VMEM((LOCAL, 128), f32),
            pltpu.VMEM((BS, 128), f32),
            pltpu.VMEM((8, 128), f32),
            pltpu.VMEM((2, BS, BS), bf16),
            pltpu.SemaphoreType.DMA((2,)),
            pltpu.SMEM((1,), i32),
        ],
        input_output_aliases=aliases,
        compiler_params=params(),
        name=f"sweep_{base}",
    )(*operands)


def load_pair(slot, x_ref, y_refs, x_buf, y_buf, sems):
    rows = pl.ds(pl.multiple_of((slot % BPD) * BS, BS), BS)
    fetch = pltpu.make_async_copy(x_ref.at[rows, :], x_buf, sems.at[0])
    fetch.start()
    fetch.wait()
    for n in range(YBLOCKS):

        @pl.when(slot // BPD == n)
        def _():
            source = y_refs[0].at[n] if n < BPD else y_refs[n - BPD + 1]
            fetch = pltpu.make_async_copy(source, y_buf, sems.at[1])
            fetch.start()
            fetch.wait()


def next_potential(now, half, total, log_count):
    return 0.5 * (now + half + entropy_weight * (log_count - log_two * total))


def fetch_terms(kept_ref, terms_ref, sems, live):
    def term_copy(n):
        return pltpu.make_async_copy(kept_ref.at[n], terms_ref.at[n], sems.at[n])

    for n in range(MOST):

        @pl.when(n < live)
        def _():
            term_copy(n).start()

    return term_copy


def columns_kernel(list_ref, live_ref, use_ref, left_ref, *refs, log_count, accs):
    acc_refs = refs[:accs]
    x_rows_ref, y_rows_ref, kept_ref, slow_ref, x_ref = refs[accs : accs + 5]
    y_refs = refs[accs + 5 : accs + 6 + FAR]
    next_ref, out_ref, col_ref, weight_ref, state_ref, part_ref, x_buf, y_buf, sems, terms_ref, term_sems = refs[accs + 6 + FAR :]
    term_copy = fetch_terms(kept_ref, terms_ref, term_sems, live_ref[0])
    clear_cols(col_ref)
    total = lane_sums(acc_refs)
    state_ref[0:1, :] = jnp.where(total > 0.0, high_of(own_beta(y_rows_ref)), lowest)
    state_ref[1:2, :] = total
    for n in range(SLOTS):

        @pl.when((use_ref[n] > 0) & (left_ref[n] < 0.0))
        def _():
            fetch = pltpu.make_async_copy(slow_ref.at[n], part_ref, sems.at[0])
            fetch.start()
            fetch.wait()
            add_part(part_ref, state_ref, n % BPD)

    half = x_rows_ref[1:2, :]
    f_next = next_potential(x_rows_ref[0:1, :], half, logs(state_ref[0:1, :], state_ref[1:2, :]), log_count)
    next_ref[0:1, :] = f_next
    next_ref[1:2, :] = half
    next_ref[2:8, :] = jnp.zeros((6, LOCAL), f32)
    alpha = (f_next - half) * scale
    state_ref[2:3, :] = alpha
    top = high_of(alpha)
    weight_ref[...] = down(jnp.exp2(alpha - top))
    reach = (top - low_of(alpha))[0, 0]

    def body(step, carry):
        slot = list_ref[step]
        y, b = slot // BPD, slot % BPD
        fits = reach <= left_ref[slot]
        term_copy(step).wait()

        @pl.when(fits)
        def _():
            sums = jnp.zeros((8, BS), f32)
            for c in range(0, BS, 64):
                weight = weight_ref[pl.ds(pl.multiple_of(b * BS + c, 64), 64), :]
                parts = [fold(terms_ref[step, c : c + 64, n : n + 128].astype(f32) * weight) for n in range(0, BS, 128)]
                sums = sums + jnp.concatenate(parts, axis=1)
            put_cols(col_ref, y, top, jnp.sum(sums, axis=0, keepdims=True))

        @pl.when(jnp.logical_not(fits))
        def _():
            load_pair(slot, x_ref, y_refs, x_buf, y_buf, sems)
            for c in range(0, BS, 128):
                row = state_ref[2:3, pl.ds(pl.multiple_of(b * BS + c, 128), 128)]
                part_ref[c : c + 128, :] = jnp.broadcast_to(row, (128, 128)).T
            shifted_cols(x_buf, y_buf, part_ref, col_ref, y)

        return carry

    lax.fori_loop(0, live_ref[0], body, 0)
    for n in range(YBLOCKS):
        out_ref[n] = logs(col_ref[n, 0:1, :], col_ref[n, 1:2, :])


def gathered(j, own_ref, came, who_ref):
    terms = [own_ref[j]] + [jnp.where(who_ref[n] == j, came(n), lowest) for n in range(PEERS)]
    top = terms[0]
    for term in terms[1:]:
        top = jnp.maximum(top, term)
    total = jnp.exp2(terms[0] - top)
    for term in terms[1:]:
        total = total + jnp.exp2(term - top)
    return top + jnp.log2(total)


def home_kernel(who_ref, peers_ref, even_in, odd_in, first_ref, second_ref, y_rows_ref, even_out, odd_out, g_ref, *, log_count):
    came = lambda n: (even_in, odd_in)[n // GROUP][n % GROUP]
    betas = []
    for j in range(BPD):
        span = slice(j * BS, (j + 1) * BS)
        half = y_rows_ref[1:2, span]
        g_next = next_potential(y_rows_ref[0:1, span], half, gathered(j, first_ref, came, who_ref), log_count)
        g_ref[0:1, span] = g_next
        betas.append((g_next - half) * scale)
        g_ref[1:2, span] = betas[j]
    g_ref[2:8, :] = jnp.zeros((6, LOCAL), f32)
    for n in range(PEERS):
        out = (even_out, odd_out)[n // GROUP]
        out[n % GROUP, 0:1, :] = jnp.where(who_ref[n] == 1, betas[1], betas[0])
        out[n % GROUP, 1:2, :] = outgoing(second_ref, peers_ref[n])


def home(who, peers, rows_in, first, second, y_rows, log_count):
    return pl.pallas_call(
        functools.partial(home_kernel, log_count=log_count),
        in_specs=[SMEM, SMEM] + [VMEM] * 5,
        out_specs=[VMEM] * 3,
        out_shape=[jax.ShapeDtypeStruct((GROUP, 2, BS), f32)] * 2 + [jax.ShapeDtypeStruct((8, LOCAL), f32)],
        compiler_params=params(),
        name="home",
    )(who, peers, *rows_in, first, second, y_rows)


def rows_kernel(list_ref, live_ref, use_ref, left_ref, from_ref, who_ref, *refs, log_count):
    even_in, odd_in, g_ref, second_ref, y_rows_ref, x_rows_ref, kept_ref, slow_ref, x_ref = refs[:9]
    y_refs = refs[9 : 10 + FAR]
    f_ref, g_out_ref, acc_ref, beta_ref, weight_ref, state_ref, part_ref, x_buf, y_buf, sems, terms_ref, term_sems = refs[10 + FAR :]
    term_copy = fetch_terms(kept_ref, terms_ref, term_sems, live_ref[0])
    shift = high_of(g_ref[1:2, :])
    acc_ref[...] = jnp.zeros((LOCAL, 128), f32)
    state_ref[0:1, :] = jnp.full((1, LOCAL), lowest, f32)
    state_ref[1:2, :] = jnp.zeros((1, LOCAL), f32)
    for n in range(BPD):
        beta_ref[n] = g_ref[1:2, n * BS : (n + 1) * BS]
    for n in range(BPD, YBLOCKS):
        source = from_ref[n]
        at = source % GROUP
        beta_ref[n] = jnp.where(source < GROUP, even_in[at, 0:1, :], odd_in[at, 0:1, :])
    weight_ref[...] = jnp.exp2(beta_ref[...] - shift)

    def body(step, carry):
        slot = list_ref[step]
        y, b = slot // BPD, slot % BPD
        beta = beta_ref[y]
        reach = jnp.maximum(high_of(beta) - shift, shift - low_of(beta))
        fits = reach[0, 0] <= left_ref[slot]
        term_copy(step).wait()

        @pl.when(fits)
        def _():
            weight = weight_ref[y]
            for c in range(0, BS, 64):
                span = pl.ds(pl.multiple_of(b * BS + c, 64), 64)
                part = acc_ref[span, :]
                for n in range(0, BS, 128):
                    part = part + terms_ref[step, c : c + 64, n : n + 128].astype(f32) * weight[:, n : n + 128]
                acc_ref[span, :] = part

        @pl.when(jnp.logical_not(fits))
        def _():
            load_pair(slot, x_ref, y_refs, x_buf, y_buf, sems)
            shifted_rows(x_buf, y_buf, beta, part_ref)
            add_part(part_ref, state_ref, b)

        return carry

    lax.fori_loop(0, live_ref[0], body, 0)
    total = lane_sums([acc_ref])
    top = jnp.where(total > 0.0, shift, lowest)
    top, total = merge(top, total, state_ref[0:1, :], state_ref[1:2, :])
    f_ref[...] = next_potential(x_rows_ref[0:1, :], x_rows_ref[1:2, :], logs(top, total), log_count)
    came = lambda n: (even_in, odd_in)[n // GROUP][n % GROUP, 1:2, :]
    total = jnp.concatenate([gathered(j, second_ref, came, who_ref) for j in range(BPD)], axis=1)
    g_next = next_potential(g_ref[0:1, :], y_rows_ref[1:2, :], total, log_count)
    g_out_ref[...] = moved_exact(g_next, y_rows_ref[2:3, :].astype(i32))


def slots_call(kernel, smem, front, kept, slow, x_blocks, y_list, outs, scratch, name):
    return pl.pallas_call(
        kernel,
        in_specs=[SMEM] * len(smem) + [VMEM] * len(front) + [HBM, HBM, ANY] + [ANY] * len(y_list),
        out_specs=[VMEM] * len(outs),
        scratch_shapes=scratch
        + [
            pltpu.VMEM((BS, 128), f32),
            pltpu.VMEM((BS, DIM), bf16),
            pltpu.VMEM((ROWS, DIM), bf16),
            pltpu.SemaphoreType.DMA((2,)),
            pltpu.VMEM((MOST, BS, BS), bf16),
            pltpu.SemaphoreType.DMA((MOST,)),
        ],
        out_shape=outs,
        compiler_params=params(),
        name=name,
    )(*smem, *front, kept, slow, x_blocks, *y_list)


def seat_tables():
    half = GROUP // 2
    offsets = np.zeros((GROUP, PEERS), np.int32)
    source = np.zeros((GROUP, YBLOCKS), np.int32)
    for seat in range(GROUP):
        odd_seat = (seat + half) % GROUP
        for other in range(GROUP):
            if other != seat and abs(other - seat) <= REACH:
                offsets[seat, other] = other - seat
            off = other - odd_seat
            if off != 0 and abs(off) <= REACH and not 0 <= seat + off < GROUP:
                offsets[seat, GROUP + other] = off
        for k, off in enumerate(ROUNDS[seat % 4]):
            source[seat, BPD + k] = list(offsets[seat]).index(off)
    index = np.full((GROUP, PEERS), -1, np.int32)
    for seat in range(GROUP):
        for k, off in enumerate(ROUNDS[seat % 4]):
            index[seat, offsets[seat] == off] = BPD + k
    return offsets, index, source


def swap(rows, devices, shift):
    groups = [[(GROUP * k + j + shift) % devices for j in range(GROUP)] for k in range(devices // GROUP)]
    return lax.all_to_all(rows, "blk", split_axis=0, concat_axis=0, tiled=True, axis_index_groups=groups)


def on_device(x_points, y_points, x_start, y_start, x_order, y_order, partners, counts):
    devices = lax.axis_size("blk")
    me = lax.axis_index("blk").astype(i32)
    log_count = math.log(LOCAL * devices)
    here = me[None]
    line = lambda v: v.reshape(1, LOCAL)

    sent = pack(here, partners, counts, line(y_order), line(x_order), y_start, x_start, y_points, x_points, devices)
    came = lax.all_to_all(sent, "blk", split_axis=0, concat_axis=0, tiled=True)
    y_rows, table, y_own, *y_sends = unpack_y(here, came, devices)
    y_far = []
    for k, block in enumerate(y_sends):
        pairs = [(i, i + ROUNDS[i % 4][k]) for i in range(devices) if 0 <= i + ROUNDS[i % 4][k] < devices]
        y_far.append(lax.ppermute(block, "blk", pairs))
    x_blocks, alpha, x_rows = unpack_x(came, table)

    offsets = lax.dynamic_slice(jnp.array(ROUNDS, i32), (me % 4, 0), (1, FAR))[0]
    live = jnp.arange(partners.shape[1], dtype=i32)[None, :] < counts[:, None]
    away = jnp.where(live, partners // BPD - me, devices)
    local_use = [((away == 0) & (partners % BPD == j)).any(axis=1) for j in range(BPD)]
    far = away[None, :, :] == offsets[:, None, None]
    use = jnp.concatenate([jnp.stack(local_use), far.any(axis=2)]).astype(i32).reshape(SLOTS)
    number = jnp.minimum(jnp.maximum(jnp.cumsum(use) - 1, 0), MOST - 1)
    count = jnp.minimum(jnp.sum(use), MOST)
    step = jnp.minimum(jnp.arange(MOST, dtype=i32), count - 1)
    at = (number[None, :] == step[:, None]) & (use[None, :] > 0)
    slots = jnp.sum(jnp.where(at, jnp.arange(SLOTS, dtype=i32)[None, :], 0), axis=1)
    lists = [slots, count[None]]

    peer_offsets, peer_index, peer_source = seat_tables()
    row = lambda t: lax.dynamic_slice(jnp.asarray(t), (me % GROUP, 0), (1, t.shape[1]))[0]
    peers, source, off = row(peer_index), row(peer_source), row(peer_offsets)
    peer = me + off
    wants = (table[:, 3 * (LOCAL // devices)] > 0.5).astype(i32)
    valid = (off != 0) & (peer >= 0) & (peer < devices)
    who = jnp.where(valid, wants[jnp.clip(peer, 0, devices - 1)], -1)

    common = (use, number, x_blocks, alpha, x_rows, y_rows)
    acc_0, *carried = sweep(common, [y_own], 0, None, None)
    acc_1, *carried = sweep(common, y_far[:2], 2, carried, None)
    acc_2, *carried = sweep(common, y_far[2:4], 4, carried, None)
    acc_3, cols_first, left, kept, slow, *rows_out = sweep(common, y_far[4:], 6, carried, peers)
    y_all = [y_own] + y_far

    even_out, odd_out = rows_out
    even_in = swap(even_out, devices, 0)
    accs = [acc_0, acc_1, acc_2, acc_3]
    x_next, cols_second = slots_call(
        functools.partial(columns_kernel, log_count=log_count, accs=len(accs)),
        lists + [use, left],
        accs + [x_rows, y_rows],
        kept,
        slow,
        x_blocks,
        y_all,
        [jax.ShapeDtypeStruct((8, LOCAL), f32), jax.ShapeDtypeStruct((YBLOCKS, 1, BS), f32)],
        [pltpu.VMEM((YBLOCKS, 8, BS), f32), pltpu.VMEM((LOCAL, 128), f32), pltpu.VMEM((8, LOCAL), f32)],
        "columns",
    )
    odd_out, cols_second = lax.optimization_barrier((odd_out, cols_second))
    rows_in = (even_in, swap(odd_out, devices, GROUP // 2))
    even_out, odd_out, g_one = home(who, peers, rows_in, cols_first, cols_second, y_rows, log_count)
    rows_in = (swap(even_out, devices, 0), swap(odd_out, devices, GROUP // 2))
    f_two, g_two = slots_call(
        functools.partial(rows_kernel, log_count=log_count),
        lists + [use, left, source, who],
        [*rows_in, g_one, cols_second, y_rows, x_next],
        kept,
        slow,
        x_blocks,
        y_all,
        [jax.ShapeDtypeStruct((1, LOCAL), f32)] * 2,
        [
            pltpu.VMEM((LOCAL, 128), f32),
            pltpu.VMEM((YBLOCKS, 1, BS), f32),
            pltpu.VMEM((YBLOCKS, 1, BS), f32),
            pltpu.VMEM((8, LOCAL), f32),
        ],
        "rows",
    )
    return f_two.reshape(LOCAL), g_two.reshape(LOCAL)


def solution(mesh):
    placed_as = (
        P("blk", None),
        P("blk", None),
        P("blk"),
        P("blk"),
        P("blk"),
        P("blk"),
        P("blk", None),
        P("blk"),
    )
    return jax.shard_map(
        on_device, mesh=mesh, in_specs=placed_as, out_specs=(P("blk"), P("blk")), check_vma=False
    )
```

profile of v0, /device:TPU:89, one launch (start us, length us, event | category | flops | bytes accessed | tf_op | source)
XLA Modules:
  0.0 401.5 jit_solution(5507485704532335029)
XLA Ops:
  0.6 14.2 %pack.1 = bf16[2048,1152]{1,0:T(8,128)(2,1)} custom-call(s32[1]{0:T(128)} %bitcast.4.me_ref, s32[2,6]{1,0:T(2,128)} %partners_ref.1, s32[2]{0:T(128)} %counts_ref.1, s32[1,2048]{1,0:T(1,128)} %bitcast.23, s32[1,2048]{1,0:T(1,128)} %bitcast.24, bf16[2048]{0:T(1024)(128)(2,1)} %y_start.1, bf16[2048]{0:T(1024)(128)(2,1)} %x_start.1, ...), custom_call_target="tpu_custom_call" | custom-call | tf_op jit(solution)/shard_map/pack/pallas_call | solution.py:177
  14.8 65.3 %all_to_all.31 = bf16[128,16,1152]{2,1,0:T(8,128)(2,1)} all-to-all(bf16[128,16,1152]{2,1,0:T(8,128)(2,1)} %bitcast.22), channel_id=1, replica_groups=mesh['blk'=128] {'blk'}, dimensions={0} | all-to-all | bytes 9437184 | tf_op jit(solution)/shard_map/all_to_all | solution.py:854
  80.1 8.0 %unpack_y.1 = (f32[8,2048]{1,0:T(8,128)}, f32[128,128]{1,0:T(8,128)}, bf16[2,1040,512]{2,1,0:T(8,128)(2,1)}, bf16[1040,512]{1,0:T(8,128)(2,1)}, bf16[1040,512]{1...) custom-call(s32[1]{0:T(128)} %bitcast.4.me_ref, ...), custom_call_target="tpu_custom_call" | custom-call | tf_op jit(solution)/shard_map/unpack_y/pallas_call | solution.py:292
  89.0 0.7 fusion.1
  89.9 0.7 collective-permute-start.1
  90.7 5.4 %collective-permute-start.2 = (bf16[1040,512]{1,0:T(8,128)(2,1)}, bf16[1040,512]{1,0:T(8,128)(2,1)}, u32[]{:S(2)}, u32[]{:S(2)}) collective-permute-start(bf16[1040,512]{1,0:T(8,128)(2,1)} %get-tuple-element.61), channel_id=1, source_target_pairs={{2,4},{3,5},{4,2},{5,3},{6,8},{7,9},{8,6},{9,7},{10,12},{11,13},{1... | collective-permute-start | bytes 3194888 | tf_op jit(solution)/shard_map/ppermute | solution.py:859
  96.1 1.9 collective-permute-start.3
  98.0 4.2 %collective-permute-start.4 = (bf16[1040,512]{1,0:T(8,128)(2,1)}, bf16[1040,512]{1,0:T(8,128)(2,1)}, u32[]{:S(2)}, u32[]{:S(2)}) collective-permute-start(bf16[1040,512]{1,0:T(8,128)(2,1)} %get-tuple-element.67), channel_id=1, source_target_pairs={{1,4},{3,6},{4,1},{5,8},{6,3},{7,10},{8,5},{9,12},{10,7},{11,14},{... | collective-permute-start | bytes 3194888 | tf_op jit(solution)/shard_map/ppermute | solution.py:859
  102.3 2.9 collective-permute-start.5
  105.2 0.7 fusion.5
  106.1 0.7 clamp_bitcast_fusion
  107.6 1.2 fusion.2.refs_10_.peers_ref
  109.0 0.7 select_reduce_fusion.list_ref
  109.8 8.5 %unpack_x.1 = (bf16[2048,512]{1,0:T(8,128)(2,1)}, f32[2048,128]{1,0:T(8,128)}, f32[8,2048]{1,0:T(8,128)}) custom-call(bf16[2048,1152]{1,0:T(8,128)(2,1)} %bitcast.21, f32[128,128]{1,0:T(8,128)} %get-tuple-element.45.table_ref), custom_call_target="tpu_custom_call" | custom-call | tf_op jit(solution)/shard_map/unpack_x/pallas_call | solution.py:337
  118.3 15.2 %sweep_0.1 = (f32[2048,128]{1,0:T(8,128)}, f32[8,1,1024]{2,1,0:T(1,128)}, f32[16]{0:T(128)}, bf16[12,1024,1024]{2,1,0:T(8,128)(2,1)}, f32[16,1024,128]{2,1,0:T(8,128)}) custom-call(s32[16]{0:T(128)} %copy-done.5, s32[16]{0:T(128)} %copy-done.6, bf16[2048,512]{1,0:T(8,128)(2,1)} %get-tuple-element.46.refs_2_.refs_8_, f32[2048,128]{1,0:T(8,128)} %get-tuple-element.47.refs_3_, ...), custom_call_target="tpu_custom_call" | custom-call | tf_op jit(solution)/shard_map/sweep_0/pallas_call | solution.py:593
  133.6 20.7 %sweep_2.1 = (f32[2048,128]{1,0:T(8,128)}, f32[8,1,1024]{2,1,0:T(1,128)}, f32[16]{0:T(128)}, bf16[12,1024,1024]{2,1,0:T(8,128)(2,1)}, f32[16,1024,128]{2,1,0:T(8,128)}) custom-call(s32[16]{0:T(128)} %copy-done.5, s32[16]{0:T(128)} %copy-done.6, bf16[2048,512]{1,0:T(8,128)(2,1)} %get-tuple-element.46.refs_2_.refs_8_, ...), custom_call_target="tpu_custom_call", output_to_operand_aliasing={{3}: (8, {}), {4}: (9, {})} | custom-call | tf_op jit(solution)/shard_map/sweep_2/pallas_call | solution.py:593
  154.3 26.1 %sweep_4.1 = (f32[2048,128]{1,0:T(8,128)}, f32[8,1,1024]{2,1,0:T(1,128)}, f32[16]{0:T(128)}, bf16[12,1024,1024]{2,1,0:T(8,128)(2,1)}, f32[16,1024,128]{2,1,0:T(8,128)}) custom-call(s32[16]{0:T(128)} %copy-done.5, s32[16]{0:T(128)} %copy-done.6, bf16[2048,512]{1,0:T(8,128)(2,1)} %get-tuple-element.46.refs_2_.refs_8_, ...), custom_call_target="tpu_custom_call", output_to_operand_aliasing={{3}: (8, {}), {4}: (9, {})} | custom-call | tf_op jit(solution)/shard_map/sweep_4/pallas_call | solution.py:593
  180.5 20.8 %sweep_6.1 = (f32[2048,128]{1,0:T(8,128)}, f32[8,1,1024]{2,1,0:T(1,128)}, f32[16]{0:T(128)}, bf16[12,1024,1024]{2,1,0:T(8,128)(2,1)}, f32[16,1024,128]{2,1,0:T(8...) custom-call(s32[16]{0:T(128)} %copy-done.5, s32[16]{0:T(128)} %copy-done.6, ...), custom_call_target="tpu_custom_call", output_to_operand_aliasing={{3}: (8, {}), {4}: (9, {})} | custom-call | tf_op jit(solution)/shard_map/sweep_6/pallas_call | solution.py:593
  201.3 85.4 %columns.1 = (f32[8,2048]{1,0:T(8,128)}, f32[8,1,1024]{2,1,0:T(1,128)}) custom-call(s32[12]{0:T(128)} %select_reduce_fusion.list_ref, s32[1]{0:T(128)} %bitcast.3.live_ref, s32[16]{0:T(128)} %copy-done.5, f32[16]{0:T(128)} %get-tuple-element.69.left_ref, f32[2048,128]{1,0:T(8,128)} %get-tuple-element.72.refs_0_, f32[2048,128]{1,0:T(8,128)} %get-tuple-element.73.refs_1_, ...), custom_call_target="tpu_custom_call" | custom-call | tf_op jit(solution)/shard_map/columns/pallas_call | solution.py:801
  286.7 3.3 all-to-all-start.2
  290.2 0.7 gather_fusion
  290.9 3.9 all-to-all-done.2.odd_in
  294.8 5.3 %all-to-all-start.1 = ((f32[8,1,1024]{2,1,0:T(1,128)}), f32[8,1,1024]{2,1,0:T(1,128)S(1)}, u32[]{:S(2)}, u32[]{:S(2)}) async-start(f32[8,1,1024]{2,1,0:T(1,128)} %get-tuple-element.70), calls=%async_computation.1 | async-start | bytes 65536 | tf_op jit(solution)/shard_map/all_to_all | solution.py:843
  300.1 1.3 bitcast_select_fusion.who_ref
  301.3 1.7 all-to-all-done.1.even_in
  303.7 1.7 home.1
  305.4 9.5 %all_to_all.32.refs_0_ = f32[8,2,1024]{2,1,0:T(2,128)} all-to-all(f32[8,2,1024]{2,1,0:T(2,128)} %get-tuple-element.82), channel_id=1, replica_groups={{0,1,2,3,4,5,6,7},{8,9,10,11,12,13,14,15},{16,17,18,19,20,21,22,23},{24..., dimensions={0} | all-to-all | bytes 131072 | tf_op jit(solution)/shard_map/all_to_all | solution.py:843
  314.9 4.1 %all-to-all-start.4 = ((f32[8,2,1024]{2,1,0:T(2,128)}), f32[8,2,1024]{2,1,0:T(2,128)S(1)}, u32[]{:S(2)}, u32[]{:S(2)}) async-start(f32[8,2,1024]{2,1,0:T(2,128)} %get-tuple-element.83), calls=%async_computation.4 | async-start | bytes 131072 | tf_op jit(solution)/shard_map/all_to_all | solution.py:843
  319.0 1.3 fusion.3.from_ref
  320.3 3.8 all-to-all-done.4.refs_1_
  324.1 0.6 copy-done.2
  324.7 76.6 %rows.1 = (f32[1,2048]{1,0:T(1,128)}, f32[1,2048]{1,0:T(1,128)}) custom-call(s32[12]{0:T(128)} %select_reduce_fusion.list_ref, s32[1]{0:T(128)} %bitcast.3.live_ref, s32[16]{0:T(128)} %copy-done.5, f32[16]{0:T(128)} %get-tuple-element.69.left_ref, s32[8]{0:T(128)} %fusion.3.from_ref, s32[16]{0:T(128)} %bitcast_select_fusion.who_ref, ...), custom_call_target="tpu_custom_call" | custom-call | tf_op jit(solution)/shard_map/rows/pallas_call | solution.py:801
  (39 shorter events, 2.6 us)
Async XLA Ops:
  80.1 8.6 %copy-start.7 = (s32[2,6]{1,0:T(2,128)S(1)}, s32[2,6]{1,0:T(2,128)}, u32[]{:S(2)}) copy-start(s32[2,6]{1,0:T(2,128)} %partners_ref.1) | copy-start | bytes 148
  80.1 8.6 %copy-start.8 = (s32[2]{0:T(128)S(1)}, s32[2]{0:T(128)}, u32[]{:S(2)}) copy-start(s32[2]{0:T(128)} %counts_ref.1) | copy-start | bytes 28
  88.1 14.2 %collective-permute-start = (bf16[1040,512]{1,0:T(8,128)(2,1)}, bf16[1040,512]{1,0:T(8,128)(2,1)S(1)}, u32[]{:S(2)}, u32[]{:S(2)}) collective-permute-start(bf16[1040,512]{1,0:T(8,128)(2,1)} %get-tuple-element.55), channel_id=1, source_target_pairs={{0,1},{1,0},{2,3},{3,2},{4,5},{5,4},{6,7},{7,6},{8,9},{9,8},{10,11... | collective-permute-start | bytes 3194888 | tf_op jit(solution)/shard_map/ppermute | solution.py:859
  89.9 43.6 %collective-permute-start.1 = (bf16[1040,512]{1,0:T(8,128)(2,1)}, bf16[1040,512]{1,0:T(8,128)(2,1)}, u32[]{:S(2)}, u32[]{:S(2)}) collective-permute-start(bf16[1040,512]{1,0:T(8,128)(2,1)} %get-tuple-element.56), channel_id=1, source_target_pairs={{0,2},{1,3},{2,0},{3,1},{4,6},{5,7},{6,4},{7,5},{8,10},{9,11},{10,... | collective-permute-start | bytes 3194888 | tf_op jit(solution)/shard_map/ppermute | solution.py:859
  90.7 63.6 %collective-permute-start.2 = (bf16[1040,512]{1,0:T(8,128)(2,1)}, bf16[1040,512]{1,0:T(8,128)(2,1)}, u32[]{:S(2)}, u32[]{:S(2)}) collective-permute-start(bf16[1040,512]{1,0:T(8,128)(2,1)} %get-tuple-element.61), channel_id=1, source_target_pairs={{2,4},{3,5},{4,2},{5,3},{6,8},{7,9},{8,6},{9,7},{10,12},{11,13},{1... | collective-permute-start | bytes 3194888 | tf_op jit(solution)/shard_map/ppermute | solution.py:859
  96.1 58.2 %collective-permute-start.3 = (bf16[1040,512]{1,0:T(8,128)(2,1)}, bf16[1040,512]{1,0:T(8,128)(2,1)}, u32[]{:S(2)}, u32[]{:S(2)}) collective-permute-start(bf16[1040,512]{1,0:T(8,128)(2,1)} %get-tuple-element.62), channel_id=1, source_target_pairs={{0,3},{2,5},{3,0},{4,7},{5,2},{6,9},{7,4},{8,11},{9,6},{10,13},{11... | collective-permute-start | bytes 3194888 | tf_op jit(solution)/shard_map/ppermute | solution.py:859
  98.0 82.4 %collective-permute-start.4 = (bf16[1040,512]{1,0:T(8,128)(2,1)}, bf16[1040,512]{1,0:T(8,128)(2,1)}, u32[]{:S(2)}, u32[]{:S(2)}) collective-permute-start(bf16[1040,512]{1,0:T(8,128)(2,1)} %get-tuple-element.67), channel_id=1, source_target_pairs={{1,4},{3,6},{4,1},{5,8},{6,3},{7,10},{8,5},{9,12},{10,7},{11,14},{... | collective-permute-start | bytes 3194888 | tf_op jit(solution)/shard_map/ppermute | solution.py:859
  102.3 16.0 %copy-start = (bf16[1040,512]{1,0:T(8,128)(2,1)}, bf16[1040,512]{1,0:T(8,128)(2,1)S(1)}, u32[]{:S(2)}) copy-start(bf16[1040,512]{1,0:T(8,128)(2,1)S(1)} %collective-permute-done.refs_10_) | copy-start | bytes 3194884
  102.3 78.2 %collective-permute-start.5 = (bf16[1040,512]{1,0:T(8,128)(2,1)}, bf16[1040,512]{1,0:T(8,128)(2,1)}, u32[]{:S(2)}, u32[]{:S(2)}) collective-permute-start(bf16[1040,512]{1,0:T(8,128)(2,1)} %get-tuple-element.68), channel_id=1, source_target_pairs={{1,2},{2,1},{3,4},{4,3},{5,6},{6,5},{7,8},{8,7},{9,10},{10,9},{11,... | collective-permute-start | bytes 3194888 | tf_op jit(solution)/shard_map/ppermute | solution.py:859
  106.0 12.3 %copy-start.5 = (s32[16]{0:T(128)}, s32[16]{0:T(128)S(1)}, u32[]{:S(2)}) copy-start(s32[16]{0:T(128)S(1)} %reshape.118.refs_0_.use_ref) | copy-start | bytes 196
  109.0 9.3 %copy-start.6 = (s32[16]{0:T(128)}, s32[16]{0:T(128)S(1)}, u32[]{:S(2)}) copy-start(s32[16]{0:T(128)S(1)} %clamp_reduce_fusion.refs_1_) | copy-start | bytes 196
  201.3 88.8 %copy-start.1 = (f32[128,128]{1,0:T(8,128)S(1)}, f32[128,128]{1,0:T(8,128)}, u32[]{:S(2)}) copy-start(f32[128,128]{1,0:T(8,128)} %get-tuple-element.45.table_ref) | copy-start | bytes 196612
  286.7 8.1 %all-to-all-start.2 = ((f32[8,1,1024]{2,1,0:T(1,128)}), f32[8,1,1024]{2,1,0:T(1,128)S(1)}, u32[]{:S(2)}, u32[]{:S(2)}) async-start(f32[8,1,1024]{2,1,0:T(1,128)} %get-tuple-element.79), calls=%async_computation.2 | async-start | bytes 65536 | tf_op jit(solution)/shard_map/all_to_all | solution.py:843
  294.8 8.3 %copy-start.3 = (f32[8,1,1024]{2,1,0:T(1,128)}, f32[8,1,1024]{2,1,0:T(1,128)S(1)}, u32[]{:S(2)}) copy-start(f32[8,1,1024]{2,1,0:T(1,128)S(1)} %all-to-all-done.2.odd_in) | copy-start | bytes 98308
  294.8 8.3 %all-to-all-start.1 = ((f32[8,1,1024]{2,1,0:T(1,128)}), f32[8,1,1024]{2,1,0:T(1,128)S(1)}, u32[]{:S(2)}, u32[]{:S(2)}) async-start(f32[8,1,1024]{2,1,0:T(1,128)} %get-tuple-element.70), calls=%async_computation.1 | async-start | bytes 65536 | tf_op jit(solution)/shard_map/all_to_all | solution.py:843
  303.1 0.6 copy-start.4
  314.9 9.2 %all-to-all-start.4 = ((f32[8,2,1024]{2,1,0:T(2,128)}), f32[8,2,1024]{2,1,0:T(2,128)S(1)}, u32[]{:S(2)}, u32[]{:S(2)}) async-start(f32[8,2,1024]{2,1,0:T(2,128)} %get-tuple-element.83), calls=%async_computation.4 | async-start | bytes 131072 | tf_op jit(solution)/shard_map/all_to_all | solution.py:843
  324.1 0.6 copy-start.2
where the time goes:
time: 408 us; the launch traced here: 401 us
  Pallas kernels  277 us (68%)
  blocking collectives  74.8 us (18%)
  starting transfers between devices  28.4 us (7%)
  waiting for transfers between devices  9.51 us (2%)
  local copies, waits for them, and re-layouts  5.62 us (1%)
  other arithmetic  4.22 us (1%)
    pallas_call x2, Pallas kernels, slots_call(): pl.pallas_call(kernel, in_specs=[SMEM] * len(smem) + [VMEM] * len(front)...  162 us
    pallas_call x4, Pallas kernels, sweep(): pl.pallas_call(functools.partial(sweep_kernel, base=base, count=count, fi...  82.9 us
    all_to_all x1, blocking collectives, on_device(): came = lax.all_to_all(sent, 'blk', split_axis=0, concat_axis=0, tiled=True)  65.3 us
    ppermute x6, starting transfers between devices, on_device(): y_far.append(lax.ppermute(block, 'blk', pairs))  15.8 us
    pallas_call x1, Pallas kernels, pack(): pl.pallas_call(functools.partial(pack_kernel, devices=devices), grid=(LOC...  14.2 us
    all_to_all x3, starting transfers between devices, swap(): lax.all_to_all(rows, 'blk', split_axis=0, concat_axis=0, tiled=True, axis...  12.6 us
    all_to_all x1, blocking collectives, swap(): lax.all_to_all(rows, 'blk', split_axis=0, concat_axis=0, tiled=True, axis...  9.52 us
    all_to_all x3, waiting for transfers between devices, swap(): lax.all_to_all(rows, 'blk', split_axis=0, concat_axis=0, tiled=True, axis...  9.49 us
  transfers between devices with their start and end apart: 9, of which 3 were waited for; matrix products, arithmetic and copies ran while one was open for 2% of the time, Pallas kernels for 18%

commit v1 on v0

--- a/solution.py
+++ b/solution.py
@@ -15,12 +15,13 @@
 REACH = 3
 LOCAL = BPD * BS
 EXTRA = 128
-WIDE = 2 * DIM + EXTRA
+WIDE = DIM + EXTRA
 TAIL = 16
 ROWS = BS + TAIL
 CHUNK = 512
 PART = 256
-ROUNDS = ((1, 2, -2, 3, -3, -1), (-1, 2, -2, -3, 3, 1), (1, -2, 2, 3, -3, -1), (-1, -2, 2, -3, 3, 1))
+ROUNDS = ((1, 3, -1, -2, -3, 2), (-1, -3, 1, -2, 3, 2), (1, 3, -1, 2, -3, -2), (-1, -3, 1, 2, 3, -2))
+EARLY = 3
 FAR = len(ROUNDS[0])
 YBLOCKS = BPD + FAR
 SLOTS = BPD * YBLOCKS
@@ -63,7 +64,7 @@
 
 
 def params():
-    return pltpu.CompilerParams(vmem_limit_bytes=62 * mebi)
+    return pltpu.CompilerParams(vmem_limit_bytes=63 * mebi)
 
 
 def whole(shape):
@@ -134,8 +135,8 @@
     return out
 
 
-def pack_kernel(
-    me_ref, partners_ref, counts_ref, y_order, x_order, y_start, x_start, y_points, x_points, out_ref, pos_ref, table_ref,
+def pack_y_kernel(
+    me_ref, partners_ref, counts_ref, y_order, x_order, y_start, x_start, points, out_ref, x_pos_ref, pos_ref, table_ref,
     *, devices
 ):
     step = pl.program_id(0)
@@ -145,8 +146,8 @@
     def _():
         y_pos, y_table = plan(y_order[...], y_start[...].astype(f32).reshape(1, LOCAL), devices, 0)
         x_pos, x_table = plan(x_order[...], x_start[...].astype(f32).reshape(1, LOCAL), devices, X_LANES)
-        pos_ref[0:1, :] = y_pos
-        pos_ref[1:2, :] = x_pos
+        pos_ref[...] = y_pos
+        x_pos_ref[...] = x_pos
         me = me_ref[0]
         offsets = partner_offsets(me)
         need = [jnp.int32(0)] * FAR
@@ -164,26 +165,43 @@
         table_ref[...] = table
 
     base = step * CHUNK
-    for n, points in enumerate((y_points, x_points)):
-        hot = ones_where(iota((CHUNK, LOCAL), 0) + base == pos_ref[n : n + 1, :])
-        out_ref[:, n * DIM : (n + 1) * DIM] = dot(hot, points[...]).astype(bf16)
+    hot = ones_where(iota((CHUNK, LOCAL), 0) + base == pos_ref[...])
+    out_ref[:, :DIM] = dot(hot, points[...]).astype(bf16)
     some = CHUNK // share
     table = table_ref[pl.ds(pl.multiple_of(step * some, some), some), :]
-    out_ref[:, 2 * DIM :] = jnp.broadcast_to(table[:, None, :], (some, share, EXTRA)).reshape(CHUNK, EXTRA).astype(bf16)
-
-
-def pack(me, partners, counts, y_order, x_order, y_start, x_start, y_points, x_points, devices):
+    out_ref[:, DIM:] = jnp.broadcast_to(table[:, None, :], (some, share, EXTRA)).reshape(CHUNK, EXTRA).astype(bf16)
+
+
+def pack_y(me, partners, counts, y_order, x_order, y_start, x_start, points, devices):
     row = whole((1, LOCAL))
     return pl.pallas_call(
-        functools.partial(pack_kernel, devices=devices),
+        functools.partial(pack_y_kernel, devices=devices),
         grid=(LOCAL // CHUNK,),
-        in_specs=[SMEM, SMEM, SMEM, row, row, whole((LOCAL,)), whole((LOCAL,)), whole((LOCAL, DIM)), whole((LOCAL, DIM))],
-        out_specs=pl.BlockSpec((CHUNK, WIDE), lambda t: (t, 0)),
-        out_shape=pltpu.HBM((LOCAL, WIDE), bf16),
-        scratch_shapes=[pltpu.VMEM((8, LOCAL), i32), pltpu.VMEM((devices, EXTRA), f32)],
+        in_specs=[SMEM, SMEM, SMEM, row, row, whole((LOCAL,)), whole((LOCAL,)), whole((LOCAL, DIM))],
+        out_specs=[pl.BlockSpec((CHUNK, WIDE), lambda t: (t, 0)), row],
+        out_shape=[pltpu.HBM((LOCAL, WIDE), bf16), jax.ShapeDtypeStruct((1, LOCAL), i32)],
+        scratch_shapes=[pltpu.VMEM((1, LOCAL), i32), pltpu.VMEM((devices, EXTRA), f32)],
         compiler_params=params(),
-        name="pack",
-    )(me, partners, counts, y_order, x_order, y_start, x_start, y_points, x_points)
+        name="pack_y",
+    )(me, partners, counts, y_order, x_order, y_start, x_start, points)
+
+
+def pack_x_kernel(pos_ref, points_ref, out_ref):
+    base = pl.program_id(0) * CHUNK
+    hot = ones_where(iota((CHUNK, LOCAL), 0) + base == pos_ref[...])
+    out_ref[...] = dot(hot, points_ref[...]).astype(bf16)
+
+
+def pack_x(pos, points):
+    return pl.pallas_call(
+        pack_x_kernel,
+        grid=(LOCAL // CHUNK,),
+        in_specs=[whole((1, LOCAL)), whole((LOCAL, DIM))],
+        out_specs=pl.BlockSpec((CHUNK, DIM), lambda t: (t, 0)),
+        out_shape=pltpu.HBM((LOCAL, DIM), bf16),
+        compiler_params=params(),
+        name="pack_x",
+    )(pos, points)
 
 
 WINDOW = PART + 16
@@ -206,7 +224,7 @@
     held, sems, own_sem, points_buf, extra_buf, in_sems = rest[FAR:]
     share = LOCAL // devices
     me = me_ref[0]
-    extra_in = pltpu.make_async_copy(came_ref.at[:, pl.ds(2 * DIM, EXTRA)], extra_buf, in_sems.at[0])
+    extra_in = pltpu.make_async_copy(came_ref.at[:, pl.ds(DIM, EXTRA)], extra_buf, in_sems.at[0])
     points_in = pltpu.make_async_copy(came_ref.at[:, pl.ds(0, DIM)], points_buf, in_sems.at[1])
     extra_in.start()
     points_in.start()
@@ -337,7 +355,7 @@
     return pl.pallas_call(
         unpack_x_kernel,
         grid=(LOCAL // CHUNK,),
-        in_specs=[pl.BlockSpec((LOCAL, DIM), lambda t: (0, 1)), whole((EXTRA, EXTRA))],
+        in_specs=[whole((LOCAL, DIM)), whole((EXTRA, EXTRA))],
         out_specs=[
             pl.BlockSpec((CHUNK, DIM), lambda t: (t, 0)),
             pl.BlockSpec((CHUNK, 128), lambda t: (t, 0)),
@@ -432,22 +450,22 @@
     return (y_rows_ref[0:1, :] - y_rows_ref[1:2, :]) * scale
 
 
-def sweep_kernel(*refs, base, count, first, last):
+def sweep_kernel(*refs, base, count, first, sends):
     use_ref, seat_of_ref, x_ref, alpha_ref, x_rows_ref, y_rows_ref = refs[:6]
     refs = refs[6:]
     if not first:
         cols_in, left_in = refs[:2]
         refs = refs[4:]
-    if last:
+    if sends is not None:
         peers_ref = refs[0]
         refs = refs[1:]
     y_refs = refs[:1] if first else refs[:count]
     refs = refs[len(y_refs) :]
     acc_ref, cols_ref, left_ref, kept_ref, slow_ref = refs[:5]
     refs = refs[5:]
-    if last:
-        group_outs = refs[:2]
-        refs = refs[2:]
+    if sends is not None:
+        group_out = refs[0]
+        refs = refs[1:]
     y_buf, sems, col_ref, weight_ref, part_ref, stat_ref, tiles, tile_sems, tile_count = refs
 
     def copy(n):
@@ -555,17 +573,17 @@
         def _():
             tile_copy(n, 0).wait()
 
-    if last:
-        for n in range(PEERS):
-            group_outs[n // GROUP][n % GROUP] = outgoing(cols_ref, peers_ref[n])
+    if sends is not None:
+        for n in range(GROUP):
+            group_out[n] = outgoing(cols_ref, peers_ref[sends * GROUP + n])
 
 
 def outgoing(cols_ref, index):
     return jnp.where(index < 0, lowest, cols_ref[jnp.maximum(index, 0)])
 
 
-def sweep(common, y_list, base, carried, peers):
-    first, last = carried is None, peers is not None
+def sweep(common, y_list, base, carried, peers=None, sends=None):
+    first = carried is None
     count = BPD if first else len(y_list)
     in_specs = [SMEM, SMEM] + [VMEM] * 4
     operands = list(common)
@@ -574,7 +592,7 @@
         in_specs += [VMEM, SMEM, HBM, HBM]
         operands += list(carried)
         aliases = {8: 3, 9: 4}
-    if last:
+    if sends is not None:
         in_specs.append(SMEM)
         operands.append(peers)
     in_specs += [ANY] * len(y_list)
@@ -587,11 +605,11 @@
         pltpu.HBM((MOST, BS, BS), bf16),
         pltpu.HBM((SLOTS, BS, 128), f32),
     ]
-    if last:
-        out_specs += [VMEM] * 2
-        out_shape += [jax.ShapeDtypeStruct((GROUP, 1, BS), f32)] * 2
+    if sends is not None:
+        out_specs.append(VMEM)
+        out_shape.append(jax.ShapeDtypeStruct((GROUP, 1, BS), f32))
     return pl.pallas_call(
-        functools.partial(sweep_kernel, base=base, count=count, first=first, last=last),
+        functools.partial(sweep_kernel, base=base, count=count, first=first, sends=sends),
         in_specs=in_specs,
         out_specs=out_specs,
         out_shape=out_shape,
@@ -850,14 +868,21 @@
     here = me[None]
     line = lambda v: v.reshape(1, LOCAL)
 
-    sent = pack(here, partners, counts, line(y_order), line(x_order), y_start, x_start, y_points, x_points, devices)
-    came = lax.all_to_all(sent, "blk", split_axis=0, concat_axis=0, tiled=True)
-    y_rows, table, y_own, *y_sends = unpack_y(here, came, devices)
-    y_far = []
-    for k, block in enumerate(y_sends):
+    y_sent, x_pos = pack_y(here, partners, counts, line(y_order), line(x_order), y_start, x_start, y_points, devices)
+    y_came = lax.all_to_all(y_sent, "blk", split_axis=0, concat_axis=0, tiled=True)
+    x_sent = pack_x(x_pos, x_points)
+    x_came = lax.all_to_all(x_sent, "blk", split_axis=0, concat_axis=0, tiled=True)
+    y_came, x_sent = lax.optimization_barrier((y_came, x_sent))
+    y_rows, table, y_own, *y_sends = unpack_y(here, y_came, devices)
+
+    def far_block(k):
         pairs = [(i, i + ROUNDS[i % 4][k]) for i in range(devices) if 0 <= i + ROUNDS[i % 4][k] < devices]
-        y_far.append(lax.ppermute(block, "blk", pairs))
-    x_blocks, alpha, x_rows = unpack_x(came, table)
+        return lax.ppermute(y_sends[k], "blk", pairs)
+
+    y_far = [far_block(k) for k in range(EARLY)]
+    x_came, y_far[1:], y_sends[EARLY:] = lax.optimization_barrier((x_came, y_far[1:], y_sends[EARLY:]))
+    y_far += [far_block(k) for k in range(EARLY, FAR)]
+    x_blocks, alpha, x_rows = unpack_x(x_came, table)
 
     offsets = lax.dynamic_slice(jnp.array(ROUNDS, i32), (me % 4, 0), (1, FAR))[0]
     live = jnp.arange(partners.shape[1], dtype=i32)[None, :] < counts[:, None]
@@ -881,13 +906,13 @@
     who = jnp.where(valid, wants[jnp.clip(peer, 0, devices - 1)], -1)
 
     common = (use, number, x_blocks, alpha, x_rows, y_rows)
-    acc_0, *carried = sweep(common, [y_own], 0, None, None)
-    acc_1, *carried = sweep(common, y_far[:2], 2, carried, None)
-    acc_2, *carried = sweep(common, y_far[2:4], 4, carried, None)
-    acc_3, cols_first, left, kept, slow, *rows_out = sweep(common, y_far[4:], 6, carried, peers)
+    acc_0, *carried = sweep(common, [y_own], 0, None)
+    acc_1, *carried = sweep(common, y_far[:EARLY], BPD, carried)
+    acc_2, *carried, odd_out = sweep(common, y_far[EARLY:-1], BPD + EARLY, carried, peers, 1)
+    acc_3, cols_first, left, kept, slow, even_out = sweep(common, y_far[-1:], YBLOCKS - 1, carried, peers, 0)
     y_all = [y_own] + y_far
 
-    even_out, odd_out = rows_out
+    odd_in = swap(odd_out, devices, GROUP // 2)
     even_in = swap(even_out, devices, 0)
     accs = [acc_0, acc_1, acc_2, acc_3]
     x_next, cols_second = slots_call(
@@ -902,9 +927,7 @@
         [pltpu.VMEM((YBLOCKS, 8, BS), f32), pltpu.VMEM((LOCAL, 128), f32), pltpu.VMEM((8, LOCAL), f32)],
         "columns",
     )
-    odd_out, cols_second = lax.optimization_barrier((odd_out, cols_second))
-    rows_in = (even_in, swap(odd_out, devices, GROUP // 2))
-    even_out, odd_out, g_one = home(who, peers, rows_in, cols_first, cols_second, y_rows, log_count)
+    even_out, odd_out, g_one = home(who, peers, (even_in, odd_in), cols_first, cols_second, y_rows, log_count)
     rows_in = (swap(even_out, devices, 0), swap(odd_out, devices, GROUP // 2))
     f_two, g_two = slots_call(
         functools.partial(rows_kernel, log_count=log_count),

time: 408 us -> 416 us (1.020)
  the two profiles are of different devices: /device:TPU:89 before, /device:TPU:112 now
where the time goes in v1:
time: 416 us; the launch traced here: 419 us
  Pallas kernels  281 us (68%)
  waiting for transfers between devices  62.3 us (15%)
  starting transfers between devices  56.2 us (14%)
  blocking collectives  7.99 us (2%)
  local copies, waits for them, and re-layouts  5.6 us (1%)
  other arithmetic  4.23 us (1%)
    pallas_call x2, Pallas kernels, slots_call(): pl.pallas_call(kernel, in_specs=[SMEM] * len(smem) + [VMEM] * len(front)...  162 us
    pallas_call x4, Pallas kernels, sweep(): pl.pallas_call(functools.partial(sweep_kernel, base=base, count=count, fi...  84 us
    all_to_all x1, waiting for transfers between devices, on_device(): lax.all_to_all(y_sent, 'blk', split_axis=0, concat_axis=0, tiled=True)  23.8 us
    ppermute x6, waiting for transfers between devices, far_block(): return lax.ppermute(y_sends[k], 'blk', pairs)  20.4 us
    all_to_all x3, starting transfers between devices, swap(): lax.all_to_all(rows, 'blk', split_axis=0, concat_axis=0, tiled=True, axis...  19.6 us
    ppermute x6, starting transfers between devices, far_block(): return lax.ppermute(y_sends[k], 'blk', pairs)  16.3 us
    all_to_all x1, waiting for transfers between devices, on_device(): lax.all_to_all(x_sent, 'blk', split_axis=0, concat_axis=0, tiled=True)  10.7 us
    all_to_all x1, starting transfers between devices, on_device(): lax.all_to_all(x_sent, 'blk', split_axis=0, concat_axis=0, tiled=True)  10.2 us
  transfers between devices with their start and end apart: 11, of which 4 were waited for; matrix products, arithmetic and copies ran while one was open for 2% of the time, Pallas kernels for 46%

profile of v1, /device:TPU:112, one launch (start us, length us, event | category | flops | bytes accessed | tf_op | source)
XLA Modules:
  0.0 418.8 jit_solution(11050373978071167858)
XLA Ops:
  0.6 9.0 %pack_y.1 = (bf16[2048,640]{1,0:T(8,128)(2,1)}, s32[1,2048]{1,0:T(1,128)}) custom-call(s32[1]{0:T(128)} %bitcast.4.me_ref, s32[2,6]{1,0:T(2,128)} %partners_ref.1, s32[2]{0:T(128)} %counts_ref.1, s32[1,2048]{1,0:T(1,128)} %bitcast.24, s32[1,2048]{1,0:T(1,128)} %bitcast.25, bf16[2048]{0:T(1024)(128)(2,1)} %y_start.1, bf16[2048]{0:T(1024)(128)(2,1)} %x_start.1, ...), custom_call_target="tpu_custom_call" | custom-call | tf_op jit(solution)/shard_map/pack_y/pallas_call | solution.py:177
  9.7 10.2 %all-to-all-start.1 = ((bf16[128,16,640]{2,1,0:T(8,128)(2,1)}), bf16[128,16,640]{2,1,0:T(8,128)(2,1)}, u32[]{:S(2)}, u32[]{:S(2)}) async-start(bf16[128,16,640]{2,1,0:T(8,128)(2,1)} %bitcast.23), calls=%async_computation.1 | async-start | bytes 5242880 | tf_op jit(solution)/shard_map/all_to_all | solution.py:872
  19.8 7.5 %pack_x.1 = bf16[2048,512]{1,0:T(8,128)(2,1)} custom-call(s32[1,2048]{1,0:T(1,128)} %get-tuple-element.52.pos_ref, bf16[2048,512]{1,0:T(8,128)(2,1)} %points_ref.1), custom_call_target="tpu_custom_call" | custom-call | tf_op jit(solution)/shard_map/pack_x/pallas_call | solution.py:196
  27.3 23.8 %all-to-all-done.1 = bf16[128,16,640]{2,1,0:T(8,128)(2,1)} async-done(((bf16[128,16,640]{2,1,0:T(8,128)(2,1)}), bf16[128,16,640]{2,1,0:T(8,128)(2,1)}, u32[]{:S(2)}, u32[]{:S(2)}) %all-to-all-start.1) | async-done | bytes 2621472 | tf_op jit(solution)/shard_map/all_to_all | solution.py:872
  51.1 10.2 %all-to-all-start = ((bf16[128,16,512]{2,1,0:T(8,128)(2,1)}), bf16[128,16,512]{2,1,0:T(8,128)(2,1)}, u32[]{:S(2)}, u32[]{:S(2)}) async-start(bf16[128,16,512]{2,1,0:T(8,128)(2,1)} %bitcast.22), calls=%async_computation | async-start | bytes 4194304 | tf_op jit(solution)/shard_map/all_to_all | solution.py:874
  61.3 8.1 %unpack_y.1 = (f32[8,2048]{1,0:T(8,128)}, f32[128,128]{1,0:T(8,128)}, bf16[2,1040,512]{2,1,0:T(8,128)(2,1)}, bf16[1040,512]{1,0:T(8,128)(2,1)}, bf16[1040,512]{1...) custom-call(s32[1]{0:T(128)} %bitcast.4.me_ref, ...), custom_call_target="tpu_custom_call" | custom-call | tf_op jit(solution)/shard_map/unpack_y/pallas_call | solution.py:310
  69.5 2.9 collective-permute-start
  72.4 1.9 collective-permute-start.1
  76.3 10.7 %all-to-all-done = bf16[128,16,512]{2,1,0:T(8,128)(2,1)} async-done(((bf16[128,16,512]{2,1,0:T(8,128)(2,1)}), bf16[128,16,512]{2,1,0:T(8,128)(2,1)}, u32[]{:S(2)}, u32[]{:S(2)}) %all-to-all-start) | async-done | bytes 2097184 | tf_op jit(solution)/shard_map/all_to_all | solution.py:874
  87.0 20.4 %collective-permute-done.refs_11_ = bf16[1040,512]{1,0:T(8,128)(2,1)} collective-permute-done((bf16[1040,512]{1,0:T(8,128)(2,1)}, bf16[1040,512]{1,0:T(8,128)(2,1)}, u32[]{:S(2)}, u32[]{:S(2)}) %collective-permute-start) | collective-permute-done | bytes 1064992 | tf_op jit(solution)/shard_map/ppermute | solution.py:880
  107.4 3.0 collective-permute-start.3
  110.4 5.5 %collective-permute-start.4 = (bf16[1040,512]{1,0:T(8,128)(2,1)}, bf16[1040,512]{1,0:T(8,128)(2,1)}, u32[]{:S(2)}, u32[]{:S(2)}) collective-permute-start(bf16[1040,512]{1,0:T(8,128)(2,1)} %get-tuple-element.79), channel_id=1, source_target_pairs={{1,4},{3,6},{4,1},{5,8},{6,3},{7,10},{8,5},{9,12},{10,7},{11,14},{... | collective-permute-start | bytes 3194888 | tf_op jit(solution)/shard_map/ppermute | solution.py:880
  115.9 0.7 fusion.5
  116.6 2.2 collective-permute-start.5
  118.9 0.7 clamp_bitcast_fusion
  120.6 1.2 fusion.2.refs_10_.peers_ref
  122.1 0.8 select_reduce_fusion.list_ref
  122.8 8.5 %unpack_x.1 = (bf16[2048,512]{1,0:T(8,128)(2,1)}, f32[2048,128]{1,0:T(8,128)}, f32[8,2048]{1,0:T(8,128)}) custom-call(bf16[2048,512]{1,0:T(8,128)(2,1)} %bitcast.8.came_ref, f32[128,128]{1,0:T(8,128)} %get-tuple-element.61.table_ref), custom_call_target="tpu_custom_call" | custom-call | tf_op jit(solution)/shard_map/unpack_x/pallas_call | solution.py:355
  131.3 26.1 %sweep_0.1 = (f32[2048,128]{1,0:T(8,128)}, f32[8,1,1024]{2,1,0:T(1,128)}, f32[16]{0:T(128)}, bf16[12,1024,1024]{2,1,0:T(8,128)(2,1)}, f32[16,1024,128]{2,1,0:T(8,128)}) custom-call(s32[16]{0:T(128)} %copy-done.4, s32[16]{0:T(128)} %copy-done.5, bf16[2048,512]{1,0:T(8,128)(2,1)} %get-tuple-element.62.refs_2_.refs_8_, f32[2048,128]{1,0:T(8,128)} %get-tuple-element.63.refs_3_, ...), custom_call_target="tpu_custom_call" | custom-call | tf_op jit(solution)/shard_map/sweep_0/pallas_call | solution.py:611
  157.4 27.4 %sweep_2.1 = (f32[2048,128]{1,0:T(8,128)}, f32[8,1,1024]{2,1,0:T(1,128)}, f32[16]{0:T(128)}, bf16[12,1024,1024]{2,1,0:T(8,128)(2,1)}, f32[16,1024,128]{2,1,0:T(8,128)}) custom-call(s32[16]{0:T(128)} %copy-done.4, s32[16]{0:T(128)} %copy-done.5, bf16[2048,512]{1,0:T(8,128)(2,1)} %get-tuple-element.62.refs_2_.refs_8_, ...), custom_call_target="tpu_custom_call", output_to_operand_aliasing={{3}: (8, {}), {4}: (9, {})} | custom-call | tf_op jit(solution)/shard_map/sweep_2/pallas_call | solution.py:611
  184.9 15.3 %sweep_5.1 = (f32[2048,128]{1,0:T(8,128)}, f32[8,1,1024]{2,1,0:T(1,128)}, f32[16]{0:T(128)}, bf16[12,1024,1024]{2,1,0:T(8,128)(2,1)}, f32[16,1024,128]{2,1,0:T(8,128)}, /*index=5*/f32[8,1,1024]{2,1,0:T(1,128)}) custom-call(s32[16]{0:T(128)} %copy-done.4, s32[16]{0:T(128)} %copy-done.5, ...), custom_call_target="tpu_custom_call", output_to_operand_aliasing={{3}: (8, {}), {4}: (9, {})} | custom-call | tf_op jit(solution)/shard_map/sweep_5/pallas_call | solution.py:611
  200.2 6.9 %all-to-all-start.3 = ((f32[8,1,1024]{2,1,0:T(1,128)}), f32[8,1,1024]{2,1,0:T(1,128)S(1)}, u32[]{:S(2)}, u32[]{:S(2)}) async-start(f32[8,1,1024]{2,1,0:T(1,128)} %get-tuple-element.87), calls=%async_computation.3 | async-start | bytes 65536 | tf_op jit(solution)/shard_map/all_to_all | solution.py:861
  207.9 15.2 %sweep_7.1 = (f32[2048,128]{1,0:T(8,128)}, f32[8,1,1024]{2,1,0:T(1,128)}, f32[16]{0:T(128)}, bf16[12,1024,1024]{2,1,0:T(8,128)(2,1)}, f32[16,1024,128]{2,1,0:T(8,128)}, /*index=5*/f32[8,1,1024]{2,1,0:T(1,128)}) custom-call(s32[16]{0:T(128)} %copy-done.4, s32[16]{0:T(128)} %copy-done.5, ...), custom_call_target="tpu_custom_call", output_to_operand_aliasing={{3}: (8, {}), {4}: (9, {})} | custom-call | tf_op jit(solution)/shard_map/sweep_7/pallas_call | solution.py:611
  223.1 5.4 %all-to-all-start.2 = ((f32[8,1,1024]{2,1,0:T(1,128)}), f32[8,1,1024]{2,1,0:T(1,128)S(1)}, u32[]{:S(2)}, u32[]{:S(2)}) async-start(f32[8,1,1024]{2,1,0:T(1,128)} %get-tuple-element.86), calls=%async_computation.2 | async-start | bytes 65536 | tf_op jit(solution)/shard_map/all_to_all | solution.py:861
  228.5 1.2 bitcast_select_fusion.who_ref
  229.7 85.4 %columns.1 = (f32[8,2048]{1,0:T(8,128)}, f32[8,1,1024]{2,1,0:T(1,128)}) custom-call(s32[12]{0:T(128)} %select_reduce_fusion.list_ref, s32[1]{0:T(128)} %bitcast.3.live_ref, s32[16]{0:T(128)} %copy-done.4, f32[16]{0:T(128)} %get-tuple-element.85.left_ref, f32[2048,128]{1,0:T(8,128)} %get-tuple-element.89.refs_0_, f32[2048,128]{1,0:T(8,128)} %get-tuple-element.90.refs_1_, ...), custom_call_target="tpu_custom_call" | custom-call | tf_op jit(solution)/shard_map/columns/pallas_call | solution.py:819
  315.7 1.7 home.1
  317.4 8.0 %all_to_all.44.refs_0_ = f32[8,2,1024]{2,1,0:T(2,128)} all-to-all(f32[8,2,1024]{2,1,0:T(2,128)} %get-tuple-element.96), channel_id=1, replica_groups={{0,1,2,3,4,5,6,7},{8,9,10,11,12,13,14,15},{16,17,18,19,20,21,22,23},{24..., dimensions={0} | all-to-all | bytes 131072 | tf_op jit(solution)/shard_map/all_to_all | solution.py:861
  325.4 7.4 %all-to-all-start.5 = ((f32[8,2,1024]{2,1,0:T(2,128)}), f32[8,2,1024]{2,1,0:T(2,128)S(1)}, u32[]{:S(2)}, u32[]{:S(2)}) async-start(f32[8,2,1024]{2,1,0:T(2,128)} %get-tuple-element.97), calls=%async_computation.5 | async-start | bytes 131072 | tf_op jit(solution)/shard_map/all_to_all | solution.py:861
  332.8 1.3 fusion.3.from_ref
  334.1 7.4 %all-to-all-done.5.refs_1_ = f32[8,2,1024]{2,1,0:T(2,128)S(1)} async-done(((f32[8,2,1024]{2,1,0:T(2,128)}), f32[8,2,1024]{2,1,0:T(2,128)S(1)}, u32[]{:S(2)}, u32[]{:S(2)}) %all-to-all-start.5) | async-done | bytes 65568 | tf_op jit(solution)/shard_map/all_to_all | solution.py:861
  342.1 76.6 %rows.1 = (f32[1,2048]{1,0:T(1,128)}, f32[1,2048]{1,0:T(1,128)}) custom-call(s32[12]{0:T(128)} %select_reduce_fusion.list_ref, s32[1]{0:T(128)} %bitcast.3.live_ref, s32[16]{0:T(128)} %copy-done.4, f32[16]{0:T(128)} %get-tuple-element.85.left_ref, s32[8]{0:T(128)} %fusion.3.from_ref, s32[16]{0:T(128)} %bitcast_select_fusion.who_ref, ...), custom_call_target="tpu_custom_call" | custom-call | tf_op jit(solution)/shard_map/rows/pallas_call | solution.py:819
  (41 shorter events, 4.6 us)
Async XLA Ops:
  9.7 41.5 %all-to-all-start.1 = ((bf16[128,16,640]{2,1,0:T(8,128)(2,1)}), bf16[128,16,640]{2,1,0:T(8,128)(2,1)}, u32[]{:S(2)}, u32[]{:S(2)}) async-start(bf16[128,16,640]{2,1,0:T(8,128)(2,1)} %bitcast.23), calls=%async_computation.1 | async-start | bytes 5242880 | tf_op jit(solution)/shard_map/all_to_all | solution.py:872
  51.1 35.9 %all-to-all-start = ((bf16[128,16,512]{2,1,0:T(8,128)(2,1)}), bf16[128,16,512]{2,1,0:T(8,128)(2,1)}, u32[]{:S(2)}, u32[]{:S(2)}) async-start(bf16[128,16,512]{2,1,0:T(8,128)(2,1)} %bitcast.22), calls=%async_computation | async-start | bytes 4194304 | tf_op jit(solution)/shard_map/all_to_all | solution.py:874
  61.3 13.0 %copy-start.6 = (s32[2,6]{1,0:T(2,128)S(1)}, s32[2,6]{1,0:T(2,128)}, u32[]{:S(2)}) copy-start(s32[2,6]{1,0:T(2,128)} %partners_ref.1) | copy-start | bytes 148
  61.3 13.0 %copy-start.7 = (s32[2]{0:T(128)S(1)}, s32[2]{0:T(128)}, u32[]{:S(2)}) copy-start(s32[2]{0:T(128)} %counts_ref.1) | copy-start | bytes 28
  69.5 37.9 %collective-permute-start = (bf16[1040,512]{1,0:T(8,128)(2,1)}, bf16[1040,512]{1,0:T(8,128)(2,1)}, u32[]{:S(2)}, u32[]{:S(2)}) collective-permute-start(bf16[1040,512]{1,0:T(8,128)(2,1)} %get-tuple-element.55), channel_id=1, source_target_pairs={{0,3},{2,5},{3,0},{4,7},{5,2},{6,9},{7,4},{8,11},{9,6},{10,13},{11... | collective-permute-start | bytes 3194888 | tf_op jit(solution)/shard_map/ppermute | solution.py:880
  72.4 35.0 %collective-permute-start.1 = (bf16[1040,512]{1,0:T(8,128)(2,1)}, bf16[1040,512]{1,0:T(8,128)(2,1)}, u32[]{:S(2)}, u32[]{:S(2)}) collective-permute-start(bf16[1040,512]{1,0:T(8,128)(2,1)} %get-tuple-element.56), channel_id=1, source_target_pairs={{1,2},{2,1},{3,4},{4,3},{5,6},{6,5},{7,8},{8,7},{9,10},{10,9},{11,... | collective-permute-start | bytes 3194888 | tf_op jit(solution)/shard_map/ppermute | solution.py:880
  75.6 81.8 %collective-permute-start.2 = (bf16[1040,512]{1,0:T(8,128)(2,1)}, bf16[1040,512]{1,0:T(8,128)(2,1)}, u32[]{:S(2)}, u32[]{:S(2)}) collective-permute-start(bf16[1040,512]{1,0:T(8,128)(2,1)} %get-tuple-element.71), channel_id=1, source_target_pairs={{0,1},{1,0},{2,3},{3,2},{4,5},{5,4},{6,7},{7,6},{8,9},{9,8},{10,11... | collective-permute-start | bytes 3194888 | tf_op jit(solution)/shard_map/ppermute | solution.py:880
  107.4 77.5 %collective-permute-start.3 = (bf16[1040,512]{1,0:T(8,128)(2,1)}, bf16[1040,512]{1,0:T(8,128)(2,1)}, u32[]{:S(2)}, u32[]{:S(2)}) collective-permute-start(bf16[1040,512]{1,0:T(8,128)(2,1)} %get-tuple-element.78), channel_id=1, source_target_pairs={{2,4},{3,5},{4,2},{5,3},{6,8},{7,9},{8,6},{9,7},{10,12},{11,13},{1... | collective-permute-start | bytes 3194888 | tf_op jit(solution)/shard_map/ppermute | solution.py:880
  110.4 74.4 %collective-permute-start.4 = (bf16[1040,512]{1,0:T(8,128)(2,1)}, bf16[1040,512]{1,0:T(8,128)(2,1)}, u32[]{:S(2)}, u32[]{:S(2)}) collective-permute-start(bf16[1040,512]{1,0:T(8,128)(2,1)} %get-tuple-element.79), channel_id=1, source_target_pairs={{1,4},{3,6},{4,1},{5,8},{6,3},{7,10},{8,5},{9,12},{10,7},{11,14},{... | collective-permute-start | bytes 3194888 | tf_op jit(solution)/shard_map/ppermute | solution.py:880
  116.6 91.3 %collective-permute-start.5 = (bf16[1040,512]{1,0:T(8,128)(2,1)}, bf16[1040,512]{1,0:T(8,128)(2,1)}, u32[]{:S(2)}, u32[]{:S(2)}) collective-permute-start(bf16[1040,512]{1,0:T(8,128)(2,1)} %get-tuple-element.84), channel_id=1, source_target_pairs={{0,2},{1,3},{2,0},{3,1},{4,6},{5,7},{6,4},{7,5},{8,10},{9,11},{10,... | collective-permute-start | bytes 3194888 | tf_op jit(solution)/shard_map/ppermute | solution.py:880
  119.7 11.6 %copy-start.4 = (s32[16]{0:T(128)}, s32[16]{0:T(128)S(1)}, u32[]{:S(2)}) copy-start(s32[16]{0:T(128)S(1)} %reshape.120.refs_0_.use_ref) | copy-start | bytes 196
  122.0 9.3 %copy-start.5 = (s32[16]{0:T(128)}, s32[16]{0:T(128)S(1)}, u32[]{:S(2)}) copy-start(s32[16]{0:T(128)S(1)} %clamp_reduce_fusion.refs_1_) | copy-start | bytes 196
  184.8 22.2 %copy-start.1 = (f32[128,128]{1,0:T(8,128)S(1)}, f32[128,128]{1,0:T(8,128)}, u32[]{:S(2)}) copy-start(f32[128,128]{1,0:T(8,128)} %get-tuple-element.61.table_ref) | copy-start | bytes 196612
  200.2 22.9 %all-to-all-start.3 = ((f32[8,1,1024]{2,1,0:T(1,128)}), f32[8,1,1024]{2,1,0:T(1,128)S(1)}, u32[]{:S(2)}, u32[]{:S(2)}) async-start(f32[8,1,1024]{2,1,0:T(1,128)} %get-tuple-element.87), calls=%async_computation.3 | async-start | bytes 65536 | tf_op jit(solution)/shard_map/all_to_all | solution.py:861
  223.1 92.0 %copy-start.2 = (f32[8,1,1024]{2,1,0:T(1,128)}, f32[8,1,1024]{2,1,0:T(1,128)S(1)}, u32[]{:S(2)}) copy-start(f32[8,1,1024]{2,1,0:T(1,128)S(1)} %all-to-all-done.3.odd_in) | copy-start | bytes 98308
  223.1 92.0 %all-to-all-start.2 = ((f32[8,1,1024]{2,1,0:T(1,128)}), f32[8,1,1024]{2,1,0:T(1,128)S(1)}, u32[]{:S(2)}, u32[]{:S(2)}) async-start(f32[8,1,1024]{2,1,0:T(1,128)} %get-tuple-element.86), calls=%async_computation.2 | async-start | bytes 65536 | tf_op jit(solution)/shard_map/all_to_all | solution.py:861
  315.1 0.6 copy-start.3
  325.4 16.0 %all-to-all-start.5 = ((f32[8,2,1024]{2,1,0:T(2,128)}), f32[8,2,1024]{2,1,0:T(2,128)S(1)}, u32[]{:S(2)}, u32[]{:S(2)}) async-start(f32[8,2,1024]{2,1,0:T(2,128)} %get-tuple-element.97), calls=%async_computation.5 | async-start | bytes 131072 | tf_op jit(solution)/shard_map/all_to_all | solution.py:861
  341.4 0.6 copy-start
